TPU v7x, 32 devices: a whole 2x2x4 slice. The times are simulated.
32 devices in a mesh: grp: 2 (over core), dom: 16 (over z, y, x).
Axes of the slice: x: 2, y: 2, z: 4, core: 2. Of those that a mesh axis runs over, the one named last changes fastest.
Arguments:
- reduced_basis: bfloat16 [98304, 256], P(('grp', 'dom')), may hold values from -6 to 6
- tangents: bfloat16 [4096, 4096], P(('grp', 'dom')), may hold values from -1 to 2, as said below
- connectivity: int32 [20, 4096], P(None, ('grp', 'dom')), may hold values from 0 to 1151, as said below
- weights: float32 [4096], P(('grp', 'dom')), may hold values from 0.5 to 8
Outputs:
- residual_basis: bfloat16 [98304, 256], P(('grp', 'dom'))
- galerkin_tangent: float32 [256, 256], replicated
- lspg_tangent: float32 [256, 256], replicated
Inputs may be any that keep to these rules, and one draw needn't show every extreme that they name: `connectivity`: numbers below 1024 are the partition's own nodes; 1024 + k is node k of the next partition in grp+dom order; the last partition names only its own nodes. An element's node numbers lie in a range of 64, except that a partition's first element may also name node 0 and its last element node 1151. `tangents`: each tangent is symmetric, and its rows and columns 60 to 63 are zero.
All inputs are finite; a program needn't handle non-finite values.
Results may differ from a plain program's by a relative error of at most 0.0013.
Values may be sent and summed in bfloat16 or wider, within the bound.
A program may use at most 64 MiB of HBM per device.

v0:
```python
import jax
import jax.numpy as jnp
from jax import lax
from jax.sharding import PartitionSpec as P

EDOF = 64
RIM = 128


def passed_along(x, axis, by):
    peers = lax.axis_size(axis)
    pairs = [(i, i + by) for i in range(peers) if 0 <= i + by < peers]
    return lax.ppermute(x, axis, pairs)


def element_rows(nodes):
    triples = nodes.T[:, :, None] * 3 + jnp.arange(3, dtype=jnp.int32)[None, None, :]
    flattened = triples.reshape(nodes.shape[1], -1)
    padding = jnp.zeros((nodes.shape[1], EDOF - flattened.shape[1]), jnp.int32)
    return jnp.concatenate([flattened, padding], axis=1)


def project(left_rows, right_rows):
    return jnp.einsum("rc,rd->cd", left_rows, right_rows, preferred_element_type=jnp.float32)


def local(reduced_basis, tangents, connectivity, weights):
    own_rows, columns = reduced_basis.shape
    rim_rows = RIM * 3
    elem_count = weights.shape[0]
    elem_block = min(elem_count, 128)
    rim_basis = passed_along(reduced_basis[:rim_rows], ("grp", "dom"), -1)
    extended = jnp.concatenate([reduced_basis, rim_basis], axis=0)

    def add_block(step_index, assembled):
        tangent_set = tangents.reshape(elem_block, EDOF, EDOF)
        dof_rows = element_rows(connectivity)
        gathered = extended[dof_rows]
        products = jnp.einsum(
            "eij,ejc->eic", tangent_set, gathered, preferred_element_type=jnp.float32
        )
        scaled = products * weights[:, None, None]
        return assembled.at[dof_rows.reshape(-1)].add(scaled.reshape(-1, columns))

    empty = jnp.zeros((own_rows + rim_rows, columns), jnp.float32)
    assembled = lax.fori_loop(0, elem_count // elem_block, add_block, empty)
    incoming = passed_along(assembled[own_rows:], ("grp", "dom"), 1)
    inner_rows = assembled[rim_rows:own_rows].astype(jnp.bfloat16)
    galerkin_part = project(reduced_basis[rim_rows:], inner_rows)
    lspg_part = project(inner_rows, inner_rows)
    edge_rows = (assembled[:rim_rows] + incoming).astype(jnp.bfloat16)
    galerkin_part = galerkin_part + project(reduced_basis[:rim_rows], edge_rows)
    lspg_part = lspg_part + project(edge_rows, edge_rows)
    residual_rows = jnp.concatenate([edge_rows, inner_rows], axis=0)
    galerkin_sum, lspg_sum = lax.psum((galerkin_part, lspg_part), ("grp", "dom"))
    total_dofs = own_rows * lax.axis_size("grp") * lax.axis_size("dom")
    scale_factor = 1.0 / float(total_dofs)
    return (residual_rows, galerkin_sum * scale_factor, lspg_sum * scale_factor)


def solution(mesh):
    placed = (
        P(("grp", "dom"), None),
        P(("grp", "dom"), None),
        P(None, ("grp", "dom")),
        P(("grp", "dom")),
    )
    return jax.shard_map(
        local,
        mesh=mesh,
        in_specs=placed,
        out_specs=(P(("grp", "dom"), None), P(), P()),
        check_vma=False,
    )
```

profile of v0, /device:TPU:0, one launch (start us, length us, event | category | flops | bytes accessed | tf_op | source)
XLA Modules:
  0.0 261.8 jit_solution(13463082407260662395)
XLA Ops:
  7.2 0.0 all-reduce.4.cloned.1.call-start
  7.2 0.9 slice.17
  8.2 0.0 copy-start
  8.2 1.4 collective-permute-start
  9.6 0.7 multiply_bitcast_fusion
  10.3 0.1 add.67
  10.4 0.1 broadcast_add_fusion
  10.5 0.1 copy.22
  10.7 0.1 reshape.53
  10.8 0.7 compare_select_fusion
  11.4 0.1 copy.13
  11.5 0.1 reshape.58
  11.6 1.6 copy.14
  13.2 3.7 %copy.15 = bf16[128,64,64]{2,1,0:T(8,128)(2,1)} copy(bf16[128,64,64]{0,2,1:T(8,128)(2,1)S(1)} %bitcast.19) | data formatting | bytes 2097152 | tf_op jit(solution)/shard_map/while/body/eval_jaxpr/reshape | solution.py:36
  16.9 1.2 collective-permute-done
  18.1 0.0 copy-done
  18.1 1.0 pad_maximum_fusion
  19.2 0.0 copy-start.4
  19.2 32.9 %gather_fusion = bf16[8192,256]{1,0:T(8,128)(2,1)} fusion(bf16[3456,256]{1,0:T(8,128)(2,1)S(1)} %pad_maximum_fusion, s32[8192]{0:T(1024)S(1)} %broadcast_clamp_fusion), kind=kCustom, calls=%fused_computation | custom fusion | bytes 8421376 | tf_op jit(solution)/shard_map/while/body/eval_jaxpr/gather | solution.py:38
  52.1 0.0 copy-done.4
  52.1 7.3 %broadcast_multiply_fusion = f32[128,256,64]{1,2,0:T(8,128)} fusion(f32[128]{0:T(128)S(1)} %copy-done.4, bf16[128,64,64]{2,1,0:T(8,128)(2,1)} %copy.15, bf16[128,64,256]{2,1,0:T(8,128)(2,1)} %bitcast.17), kind=kOutput, calls=%fused_computation.2 | convolution fusion | flops 270532608 | bytes 13632000 | tf_op jit(solution)/shard_map/while/body/eval_jaxpr/eij,ejc->eic/dot_general | solution.py:39
  59.4 45.5 %scatter_custom_fusion = f32[3456,256]{1,0:T(8,128)S(1)} fusion(s32[8192]{0:T(1024)} %bitcast.20, f32[8192,256]{1,0:T(8,128)} %bitcast.18, f32[]{:T(128)} %constant.5.clone.1), kind=kCustom, calls=%fused_computation.5 | custom fusion | flops 2097152 | bytes 3539456 | tf_op jit(solution)/shard_map/while/body/eval_jaxpr/scatter-add | solution.py:43
  104.9 0.0 copy-start.1
  104.9 4.7 %collective-permute-start.1 = (f32[384,256]{1,0:T(8,128)S(1)}, f32[384,256]{1,0:T(8,128)S(1)}, u32[]{:S(2)}, u32[]{:S(2)}) collective-permute-start(f32[384,256]{1,0:T(8,128)S(1)} %slice.25), channel_id=1, source_target_pairs={{0,1},{1,2},{2,3},{3,4},{4,5},{5,6},{6,7},{7,8},{8,9},{9,10},{10,1... | collective-permute-start | bytes 1179656 | tf_op jit(solution)/shard_map/ppermute | solution.py:13
  109.6 0.7 fusion.8
  110.3 1.2 slice.35
  111.5 0.0 copy-done.1
  111.5 0.6 fusion.2
  112.2 3.7 %collective-permute-done.1 = f32[384,256]{1,0:T(8,128)S(1)} collective-permute-done((f32[384,256]{1,0:T(8,128)S(1)}, f32[384,256]{1,0:T(8,128)S(1)}, u32[]{:S(2)}, u32[]{:S(2)}) %collective-permute-start.1) | collective-permute-done | bytes 393248 | tf_op jit(solution)/shard_map/ppermute | solution.py:13
  115.9 0.1 fusion.5
  115.9 0.0 copy-start.3
  115.9 0.0 copy-start.2
  115.9 1.0 convolution_add_fusion
  116.9 0.0 copy-done.3
  116.9 1.0 fusion.4
  117.9 0.0 all-reduce.4.cloned.1.call-update
  117.9 0.0 copy-done.2
  117.9 2.2 pad_maximum_fusion.1
  120.1 132.1 %all-reduce.4.cloned.1.call-done = (f32[256,256]{0,1:T(8,128)}, f32[256,256]{0,1:T(8,128)}) async-done(((f32[256,256]{0,1:T(8,128)}, f32[256,256]{0,1:T(8,128)}), (f32[256,256]{0,1:T(8,128)}, f32[256,256]{0,1:T(8,128)})) %all-reduce.4.cloned.1.call-update) | async-done | bytes 524304 | tf_op jit(solution)/shard_map/psum | solution.py:55
  252.2 1.1 broadcast_multiply_fusion.1
  253.3 0.8 copy.19
  254.1 0.8 copy.18
  (7 shorter events, 0.1 us)
Async XLA Ops:
  7.2 245.0 %all-reduce.4.cloned.1.call-start = ((), (), s32[]{:S(2)}) async-start(), calls=%async_computation | async-start | bytes 1048576 | tf_op jit(solution)/shard_map/psum | solution.py:55
  8.2 10.0 %copy-start = (bf16[3072,256]{1,0:T(8,128)(2,1)S(1)}, bf16[3072,256]{1,0:T(8,128)(2,1)}, u32[]{:S(2)}) copy-start(bf16[3072,256]{1,0:T(8,128)(2,1)} %param.4) | copy-start | bytes 4718596
  8.2 10.0 %collective-permute-start = (bf16[384,256]{1,0:T(8,128)(2,1)S(1)}, bf16[384,256]{1,0:T(8,128)(2,1)}, u32[]{:S(2)}, u32[]{:S(2)}) collective-permute-start(bf16[384,256]{1,0:T(8,128)(2,1)S(1)} %slice.17), channel_id=1, source_target_pairs={{1,0},{2,1},{3,2},{4,3},{5,4},{6,5},{7,6},{8,7},{9,8},{10,9},{11,1... | collective-permute-start | bytes 589832 | tf_op jit(solution)/shard_map/ppermute | solution.py:13
  19.2 32.9 %copy-start.4 = (f32[128]{0:T(128)S(1)}, f32[128]{0:T(128)}, u32[]{:S(2)}) copy-start(f32[128]{0:T(128)} %param.7) | copy-start | bytes 1540
  104.9 6.6 %copy-start.1 = (bf16[3072,256]{1,0:T(8,128)(2,1)S(1)}, bf16[3072,256]{1,0:T(8,128)(2,1)}, u32[]{:S(2)}) copy-start(bf16[3072,256]{1,0:T(8,128)(2,1)} %param.4) | copy-start | bytes 4718596
  104.9 10.9 %collective-permute-start.1 = (f32[384,256]{1,0:T(8,128)S(1)}, f32[384,256]{1,0:T(8,128)S(1)}, u32[]{:S(2)}, u32[]{:S(2)}) collective-permute-start(f32[384,256]{1,0:T(8,128)S(1)} %slice.25), channel_id=1, source_target_pairs={{0,1},{1,2},{2,3},{3,4},{4,5},{5,6},{6,7},{7,8},{8,9},{9,10},{10,1... | collective-permute-start | bytes 1179656 | tf_op jit(solution)/shard_map/ppermute | solution.py:13
  115.9 1.0 copy-start.3
  115.9 2.0 copy-start.2
Sparse Core Ops, SparseCore 0:
  118.0 134.1 all-reduce.3
where the time goes:
time: 262 us
  waiting for transfers between devices  137 us (52%)
  other arithmetic  51.3 us (20%)
  local copies, waits for them, and re-layouts  42.6 us (16%)
  between operations  14.2 us (5%)
  matrix products  10.5 us (4%)
  starting transfers between devices  6.15 us (2%)
    psum x1, waiting for transfers between devices, local(): lax.psum((galerkin_part, lspg_part), ('grp', 'dom'))  132 us
    scatter-add x1, other arithmetic, add_block(): return assembled.at[dof_rows.reshape(-1)].add(scaled.reshape(-1, columns))  45.5 us
    gather x1, local copies, waits for them, and re-layouts, add_block(): gathered = extended[dof_rows]  32.9 us
    dot_general x1, matrix products, add_block(): jnp.einsum('eij,ejc->eic', tangent_set, gathered, preferred_element_type=...  7.29 us
    ppermute x2, starting transfers between devices, passed_along(): return lax.ppermute(x, axis, pairs)  6.11 us
  transfers between devices with their start and end apart: 3, of which 3 were waited for; matrix products, arithmetic and copies ran while one was open for 5% of the time, Pallas kernels for 0%

commit v1 on v0

v1 whole, which is shorter than its diff:
```python
import functools

import jax
import jax.numpy as jnp
from jax import lax
from jax.experimental import pallas as pl
from jax.experimental.pallas import tpu as pltpu
from jax.sharding import PartitionSpec as P

EDOF = 64
RIM = 128
LANES = 128
GROUP = 4
MESH = pl.DeviceIdType.MESH
VMEM_LIMIT = 48 * 1024 * 1024


def passed_along(x, axis, by):
    peers = lax.axis_size(axis)
    pairs = [(i, i + by) for i in range(peers) if 0 <= i + by < peers]
    return lax.ppermute(x, axis, pairs)


def transposed_dot(left, right):
    return lax.dot_general(
        left, right, (((0,), (0,)), ((), ())), preferred_element_type=jnp.float32
    )


def assemble_kernel(
    own_rows, rim_rows, nodes_ref, weights_ref, basis_ref, rim_ref, tangents_ref,
    rows_ref, edge_ref, over_ref, *scratch,
):
    halves = basis_ref.shape[1] // LANES
    table = scratch[:halves]
    totals = [scratch[halves * (1 + u):halves * (2 + u)] for u in range(GROUP)]
    at = halves * (1 + GROUP)
    picked = [scratch[at + halves * u:at + halves * (u + 1)] for u in range(GROUP)]
    at += halves * GROUP
    products = [scratch[at + halves * u:at + halves * (u + 1)] for u in range(GROUP)]
    node_count, elem_count = nodes_ref.shape
    chunk = rim_rows
    all_rows = own_rows + rim_rows

    def widen(i, carry):
        at_rows = pl.ds(pl.multiple_of(i * chunk, chunk), chunk)
        for h in range(halves):
            table[h][at_rows, :] = basis_ref[at_rows, h * LANES:(h + 1) * LANES].astype(jnp.float32)
            for u in range(GROUP):
                totals[u][h][at_rows, :] = jnp.zeros((chunk, LANES), jnp.float32)
        return carry

    lax.fori_loop(0, own_rows // chunk, widen, 0)
    for h in range(halves):
        table[h][own_rows:all_rows, :] = rim_ref[:, h * LANES:(h + 1) * LANES].astype(jnp.float32)
        table[h][all_rows:all_rows + 8, :] = jnp.zeros((8, LANES), jnp.float32)
        for u in range(GROUP):
            totals[u][h][own_rows:all_rows + 8, :] = jnp.zeros((rim_rows + 8, LANES), jnp.float32)
    keep = lax.broadcasted_iota(jnp.int32, (8, LANES), 0) < 3

    def add_group(i, carry):
        base = i * GROUP
        starts = [[nodes_ref[k, base + u] * 3 for k in range(node_count)] for u in range(GROUP)]
        for u in range(GROUP):
            for k in range(node_count):
                for h in range(halves):
                    picked[u][h][3 * k:3 * k + 8, :] = table[h][pl.ds(starts[u][k], 8), :]
        for u in range(GROUP):
            block = jnp.concatenate([picked[u][h][:EDOF, :] for h in range(halves)], axis=1)
            product = jnp.dot(
                tangents_ref[base + u], block.astype(jnp.bfloat16),
                preferred_element_type=jnp.float32,
            ) * weights_ref[base + u]
            for h in range(halves):
                products[u][h][:EDOF, :] = product[:, h * LANES:(h + 1) * LANES]
        for k in range(node_count):
            for u in range(GROUP):
                for h in range(halves):
                    part = jnp.where(keep, products[u][h][3 * k:3 * k + 8, :], 0.0)
                    spot = pl.ds(starts[u][k], 8)
                    totals[u][h][spot, :] = totals[u][h][spot, :] + part
        return carry

    for u in range(GROUP):
        for h in range(halves):
            picked[u][h][...] = jnp.zeros(picked[u][h].shape, jnp.float32)
            products[u][h][...] = jnp.zeros(products[u][h].shape, jnp.float32)
    lax.fori_loop(0, elem_count // GROUP, add_group, 0)

    def summed(at_rows, h):
        value = totals[0][h][at_rows, :]
        for u in range(1, GROUP):
            value = value + totals[u][h][at_rows, :]
        return value

    def finish(i, carry):
        at_rows = pl.ds(pl.multiple_of(i * chunk, chunk), chunk)
        for h in range(halves):
            rows_ref[at_rows, h * LANES:(h + 1) * LANES] = summed(at_rows, h).astype(jnp.bfloat16)
        return carry

    lax.fori_loop(1, own_rows // chunk, finish, 0)
    for h in range(halves):
        lanes = slice(h * LANES, (h + 1) * LANES)
        edge = summed(pl.ds(0, rim_rows), h)
        edge_ref[:, lanes] = edge
        rows_ref[0:rim_rows, lanes] = edge.astype(jnp.bfloat16)
        over_ref[:, lanes] = summed(pl.ds(own_rows, rim_rows), h)


def assemble(basis, rim_basis, tangents, nodes, weights):
    own_rows, columns = basis.shape
    rim_rows = rim_basis.shape[0]
    halves = columns // LANES
    tall = pltpu.VMEM((own_rows + rim_rows + 8, LANES), jnp.float32)
    short = pltpu.VMEM((EDOF + 8, LANES), jnp.float32)
    vmem = pl.BlockSpec(memory_space=pltpu.VMEM)
    smem = pl.BlockSpec(memory_space=pltpu.SMEM)
    return pl.pallas_call(
        functools.partial(assemble_kernel, own_rows, rim_rows),
        out_shape=(
            jax.ShapeDtypeStruct((own_rows, columns), jnp.bfloat16),
            jax.ShapeDtypeStruct((rim_rows, columns), jnp.float32),
            jax.ShapeDtypeStruct((rim_rows, columns), jnp.float32),
        ),
        in_specs=[smem, smem, vmem, vmem, vmem],
        out_specs=(vmem, vmem, vmem),
        scratch_shapes=[tall] * (halves * (1 + GROUP)) + [short] * (halves * GROUP * 2),
        compiler_params=pltpu.CompilerParams(vmem_limit_bytes=VMEM_LIMIT),
        name="assemble",
    )(nodes, weights, basis, rim_basis, tangents)


def reduce_kernel(
    peers, factor, basis_ref, rows_ref, edge_ref, over_ref, out_ref, edge_out_ref,
    arrived, part, half, shards, mine, rim_sems, pair_sems, send_sems, recv_sems,
    spread_sems, spread_recv, pass_sems, pass_recv,
):
    g = lax.axis_index("grp")
    d = lax.axis_index("dom")
    sibling = (1 - g, d)
    rim_rows, columns = edge_ref.shape
    own_rows = basis_ref.shape[0]
    height = columns // peers
    spot = g * peers + d
    after = lax.rem(spot + 1, 2 * peers)
    before = lax.rem(spot + 2 * peers - 1, 2 * peers)
    following = (after // peers, lax.rem(after, peers))
    previous = (before // peers, lax.rem(before, peers))

    def shard(of):
        return pl.ds(pl.multiple_of(of * height, height), height)

    def peer(k):
        return lax.rem(d + k, peers)

    barrier = pltpu.get_barrier_semaphore()
    greeted = [sibling, following, previous] + [(g, peer(k)) for k in range(1, peers)]
    for device in greeted:
        pl.semaphore_signal(barrier, inc=1, device_id=device, device_id_type=MESH)
    pl.semaphore_wait(barrier, len(greeted))

    def remote(src, dst, send, recv, device):
        return pltpu.make_async_remote_copy(
            src_ref=src, dst_ref=dst, send_sem=send, recv_sem=recv,
            device_id=device, device_id_type=MESH,
        )

    rim_copy = remote(over_ref, arrived, rim_sems.at[0], rim_sems.at[1], following)
    rim_copy.start()
    part[...] = jnp.zeros(part.shape, jnp.float32)

    def project(i, carry):
        at_rows = pl.ds(pl.multiple_of(i * rim_rows, rim_rows), rim_rows)
        rows = rows_ref[at_rows, :]
        part[0] += transposed_dot(basis_ref[at_rows, :], rows)
        part[1] += transposed_dot(rows, rows)
        return carry

    lax.fori_loop(1, own_rows // rim_rows, project, 0)
    rim_copy.wait()
    edge_rows = (edge_ref[...] + arrived[...]).astype(jnp.bfloat16)
    edge_out_ref[...] = edge_rows
    part[0] += transposed_dot(basis_ref[0:rim_rows, :], edge_rows)
    part[1] += transposed_dot(edge_rows, edge_rows)

    pair_copy = remote(part.at[1 - g], half, pair_sems.at[0], pair_sems.at[1], sibling)
    pair_copy.start()
    pair_copy.wait()
    half[...] = half[...] + part[g]

    copies = []
    for k in range(1, peers):
        copy = remote(
            half.at[shard(peer(k))], shards.at[k], send_sems.at[k], recv_sems.at[k], (g, peer(k))
        )
        copy.start()
        copies.append(copy)
    total = half[shard(d), :]
    for k in range(1, peers):
        copies[k - 1].wait_recv()
        total = total + shards[k]
    mine[...] = total * factor
    for copy in copies:
        copy.wait_send()

    spreads = []
    for k in range(1, peers):
        copy = remote(
            mine, out_ref.at[g, shard(d)], spread_sems.at[k], spread_recv.at[k], (g, peer(k))
        )
        copy.start()
        spreads.append(copy)
    passes = []
    own = remote(mine, out_ref.at[g, shard(d)], pass_sems.at[0], pass_recv.at[0], sibling)
    own.start()
    passes.append(own)
    out_ref[g, shard(d), :] = mine[...]
    for k in range(1, peers):
        spreads[k - 1].wait_recv()
        source = lax.rem(d + peers - k, peers)
        place = out_ref.at[g, shard(source)]
        copy = remote(place, place, pass_sems.at[k], pass_recv.at[k], sibling)
        copy.start()
        passes.append(copy)
    for copy in spreads:
        copy.wait_send()
    for copy in passes:
        copy.wait()


def reduce_all(basis, rows, edge, over, peers, factor):
    rim_rows, columns = edge.shape
    height = columns // peers
    vmem = pl.BlockSpec(memory_space=pltpu.VMEM)
    dma = pltpu.SemaphoreType.DMA
    return pl.pallas_call(
        functools.partial(reduce_kernel, peers, factor),
        out_shape=(
            jax.ShapeDtypeStruct((2, columns, columns), jnp.float32),
            jax.ShapeDtypeStruct((rim_rows, columns), jnp.bfloat16),
        ),
        in_specs=[vmem] * 4,
        out_specs=(vmem, vmem),
        scratch_shapes=[
            pltpu.VMEM((rim_rows, columns), jnp.float32),
            pltpu.VMEM((2, columns, columns), jnp.float32),
            pltpu.VMEM((columns, columns), jnp.float32),
            pltpu.VMEM((peers, height, columns), jnp.float32),
            pltpu.VMEM((height, columns), jnp.float32),
            dma((2,)), dma((2,)), dma((peers,)), dma((peers,)),
            dma((peers,)), dma((peers,)), dma((peers,)), dma((peers,)),
        ],
        compiler_params=pltpu.CompilerParams(
            collective_id=0, has_side_effects=True, vmem_limit_bytes=VMEM_LIMIT
        ),
        name="reduce_all",
    )(basis, rows, edge, over)


def local(reduced_basis, tangents, connectivity, weights):
    own_rows, columns = reduced_basis.shape
    rim_rows = RIM * 3
    elem_count = weights.shape[0]
    groups, peers = lax.axis_size("grp"), lax.axis_size("dom")
    factor = 1.0 / float(own_rows * groups * peers)
    rim_basis = passed_along(reduced_basis[:rim_rows], ("grp", "dom"), -1)
    rows, edge, over = assemble(
        reduced_basis, rim_basis, tangents.reshape(elem_count, EDOF, EDOF), connectivity, weights
    )
    if groups == 2 and columns % peers == 0 and (columns // peers) % 8 == 0:
        both, edge_rows = reduce_all(reduced_basis, rows, edge, over, peers, factor)
        return lax.dynamic_update_slice(rows, edge_rows, (0, 0)), both[0], both[1]
    incoming = passed_along(over, ("grp", "dom"), 1)
    edge_rows = (edge + incoming).astype(jnp.bfloat16)
    rows = lax.dynamic_update_slice(rows, edge_rows, (0, 0))
    sums = lax.psum(
        (transposed_dot(reduced_basis, rows), transposed_dot(rows, rows)), ("grp", "dom")
    )
    return rows, sums[0] * factor, sums[1] * factor


def solution(mesh):
    placed = (
        P(("grp", "dom"), None),
        P(("grp", "dom"), None),
        P(None, ("grp", "dom")),
        P(("grp", "dom")),
    )
    return jax.shard_map(
        local,
        mesh=mesh,
        in_specs=placed,
        out_specs=(P(("grp", "dom"), None), P(), P()),
        check_vma=False,
    )
```

time: 262 us -> 68.6 us (0.26)
  waiting for transfers between devices: 137 us -> 3.8 us
  Pallas kernels: 0 us -> 52.9 us
  other arithmetic: 51.3 us -> 0 us
  local copies, waits for them, and re-layouts: 42.6 us -> 9.7 us
  between operations: 14.2 us -> 0.7 us
  matrix products: 10.5 us -> 0 us
  starting transfers between devices: 6.15 us -> 1.29 us
    psum x1 -> x0, waiting for transfers between devices: 132 us -> none  [local(): lax.psum((galerkin_part, lspg_part), ('grp', 'dom'))]
    pallas_call x0 -> x2, Pallas kernels: none -> 52.9 us  [the longest x1 34.8 us: reduce_all(): pl.pallas_call(functools.partial(reduce_kernel, peers, factor), out_shape...]
    scatter-add x1 -> x0, other arithmetic: 45.5 us -> none  [add_block(): return assembled.at[dof_rows.reshape(-1)].add(scaled.reshape(-1, columns))]
    gather x1 -> x0, local copies, waits for them, and re-layouts: 32.9 us -> none  [add_block(): gathered = extended[dof_rows]]
    dot_general x5 -> x0, matrix products: 10.5 us -> none  [the longest x1 7.29 us: add_block(): jnp.einsum('eij,ejc->eic', tangent_set, gathered, preferred_element_type=...]
    ppermute x2 -> x1, starting transfers between devices: 6.11 us -> 1.29 us  [passed_along(): return lax.ppermute(x, axis, pairs)]
    concatenate x2 -> x0, other arithmetic: 3.21 us -> none  [the longest x1 2.17 us: local(): residual_rows = jnp.concatenate([edge_rows, inner_rows], axis=0)]
  transfers between devices with their start and end apart: 3 -> 1, of which waited for: 3 -> 1; matrix products, arithmetic and copies ran while one was open for 5% -> 7% of each run, Pallas kernels for 0% -> 0%
where the time goes in v1:
time: 68.6 us; the launch traced here: 68.4 us
  Pallas kernels  52.9 us (77%)
  local copies, waits for them, and re-layouts  9.7 us (14%)
  waiting for transfers between devices  3.8 us (6%)
  starting transfers between devices  1.29 us (2%)
  between operations  0.7 us (1%)
    pallas_call x1, Pallas kernels, reduce_all(): pl.pallas_call(functools.partial(reduce_kernel, peers, factor), out_shape...  34.8 us
    pallas_call x1, Pallas kernels, assemble(): pl.pallas_call(functools.partial(assemble_kernel, own_rows, rim_rows), ou...  18.1 us
    unnamed x13, local copies, waits for them, and re-layouts  4.86 us
    ppermute x1, waiting for transfers between devices, passed_along(): return lax.ppermute(x, axis, pairs)  3.8 us
    reshape x1, local copies, waits for them, and re-layouts, local(): tangents.reshape(elem_count, EDOF, EDOF)  2.99 us
  transfers between devices with their start and end apart: 1, of which 1 were waited for; matrix products, arithmetic and copies ran while one was open for 7% of the time, Pallas kernels for 0%

profile of v1, /device:TPU:0, one launch (start us, length us, event | category | flops | bytes accessed | tf_op | source)
XLA Modules:
  0.0 68.4 jit_solution(15021098398176286557)
XLA Ops:
  0.6 0.9 %slice.9 = bf16[384,256]{1,0:T(8,128)(2,1)S(1)} slice(bf16[3072,256]{1,0:T(8,128)(2,1)} %basis_ref.3), slice={[0:384], [0:256]} | slice | bytes 393216 | tf_op jit(solution)/shard_map/slice | solution.py:267
  1.6 1.3 %collective-permute-start = (bf16[384,256]{1,0:T(8,128)(2,1)S(1)}, bf16[384,256]{1,0:T(8,128)(2,1)S(1)}, u32[]{:S(2)}, u32[]{:S(2)}) collective-permute-start(bf16[384,256]{1,0:T(8,128)(2,1)S(1)} %slice.9), channel_id=1, source_target_pairs={{1,0},{2,1},{3,2},{4,3},{5,4},{6,5},{7,6},{8,7},{9,8},{10,9},{11,1... | collective-permute-start | bytes 589832 | tf_op jit(solution)/shard_map/ppermute | solution.py:21
  2.9 1.6 %copy.7 = bf16[128,4096]{0,1:T(8,128)(2,1)S(1)} copy(bf16[128,4096]{1,0:T(8,128)(2,1)} %param.5) | data formatting | bytes 2097152 | tf_op args[1]
  4.5 0.0 copy-start.4
  4.5 0.0 copy-start.5
  4.5 3.0 %copy.8.tangents_ref = bf16[128,64,64]{2,1,0:T(8,128)(2,1)S(1)} copy(bf16[128,64,64]{0,2,1:T(8,128)(2,1)S(1)} %bitcast.5) | data formatting | bytes 2097152 | tf_op jit(solution)/shard_map/reshape | solution.py:269
  7.5 3.8 %collective-permute-done.rim_ref = bf16[384,256]{1,0:T(8,128)(2,1)S(1)} collective-permute-done((bf16[384,256]{1,0:T(8,128)(2,1)S(1)}, bf16[384,256]{1,0:T(8,128)(2,1)S(1)}, u32[]{:S(2)}, u32[]{:S(2)}) %collective-permute-start) | collective-permute-done | bytes 196640 | tf_op jit(solution)/shard_map/ppermute | solution.py:21
  11.3 0.0 copy-done.4
  11.3 0.0 copy-done.5
  11.3 0.0 copy-start
  11.3 1.4 %copy-done = bf16[3072,256]{1,0:T(8,128)(2,1)S(1)} copy-done((bf16[3072,256]{1,0:T(8,128)(2,1)S(1)}, bf16[3072,256]{1,0:T(8,128)(2,1)}, u32[]{:S(2)}) %copy-start) | copy-done | bytes 1572888
  12.7 0.0 copy-start.1
  12.7 18.1 %assemble.1 = (bf16[3072,256]{1,0:T(8,128)(2,1)}, f32[384,256]{1,0:T(8,128)S(1)}, f32[384,256]{1,0:T(8,128)S(1)}) custom-call(s32[20,128]{1,0:T(8,128)S(1)} %copy-done.4, f32[128]{0:T(128)S(1)} %copy-done.5, bf16[3072,256]{1,0:T(8,128)(2,1)S(1)} %copy-done, bf16[384,256]{1,0:T(8,128)(2,1)S(1)} %collective-permute-done.rim_ref, ...), custom_call_target="tpu_custom_call" | custom-call | tf_op jit(solution)/shard_map/assemble/pallas_call | solution.py:119
  30.8 0.0 copy-done.1
  30.8 0.0 copy-start.2
  30.8 1.4 %copy-done.2 = bf16[3072,256]{1,0:T(8,128)(2,1)S(1)} copy-done((bf16[3072,256]{1,0:T(8,128)(2,1)S(1)}, bf16[3072,256]{1,0:T(8,128)(2,1)}, u32[]{:S(2)}) %copy-start.2) | copy-done | bytes 1572888
  32.2 34.8 %reduce_all.1 = (f32[2,256,256]{2,1,0:T(8,128)S(1)}, bf16[384,256]{1,0:T(8,128)(2,1)S(1)}) custom-call(bf16[3072,256]{1,0:T(8,128)(2,1)S(1)} %copy-done.1, bf16[3072,256]{1,0:T(8,128)(2,1)S(1)} %copy-done.2, f32[384,256]{1,0:T(8,128)S(1)} %get-tuple-element.9.edge_ref, f32[384,256]{1,0:T(8,128)S(1)} %get-tuple-element.10.over_ref), custom_call_target="tpu_custom_call" | custom-call | tf_op jit(solution)/shard_map/reduce_all/pallas_call | solution.py:237
  67.1 0.0 copy-start.3
  67.1 0.9 %slice_bitcast_fusion = (f32[256,256]{1,0:T(8,128)}, f32[256,256]{1,0:T(8,128)}) fusion(f32[2,256,256]{2,1,0:T(8,128)S(1)} %get-tuple-element.12), kind=kLoop, calls=%fused_computation | loop fusion | bytes 1048576 | tf_op jit(solution)/shard_map/squeeze | solution.py:273
  68.0 0.4 copy-done.3
  (1 shorter events, 0.0 us)
Async XLA Ops:
  1.6 9.7 %collective-permute-start = (bf16[384,256]{1,0:T(8,128)(2,1)S(1)}, bf16[384,256]{1,0:T(8,128)(2,1)S(1)}, u32[]{:S(2)}, u32[]{:S(2)}) collective-permute-start(bf16[384,256]{1,0:T(8,128)(2,1)S(1)} %slice.9), channel_id=1, source_target_pairs={{1,0},{2,1},{3,2},{4,3},{5,4},{6,5},{7,6},{8,7},{9,8},{10,9},{11,1... | collective-permute-start | bytes 589832 | tf_op jit(solution)/shard_map/ppermute | solution.py:21
  4.5 6.8 %copy-start.4 = (s32[20,128]{1,0:T(8,128)S(1)}, s32[20,128]{1,0:T(8,128)}, u32[]{:S(2)}) copy-start(s32[20,128]{1,0:T(8,128)} %nodes_ref.1) | copy-start | bytes 30724
  4.5 6.8 %copy-start.5 = (f32[128]{0:T(128)S(1)}, f32[128]{0:T(128)}, u32[]{:S(2)}) copy-start(f32[128]{0:T(128)} %weights_ref.1) | copy-start | bytes 1540
  11.3 1.4 %copy-start = (bf16[3072,256]{1,0:T(8,128)(2,1)S(1)}, bf16[3072,256]{1,0:T(8,128)(2,1)}, u32[]{:S(2)}) copy-start(bf16[3072,256]{1,0:T(8,128)(2,1)} %basis_ref.3) | copy-start | bytes 4718596
  12.7 18.1 %copy-start.1 = (bf16[3072,256]{1,0:T(8,128)(2,1)S(1)}, bf16[3072,256]{1,0:T(8,128)(2,1)}, u32[]{:S(2)}) copy-start(bf16[3072,256]{1,0:T(8,128)(2,1)} %basis_ref.3) | copy-start | bytes 4718596
  30.8 1.4 %copy-start.2 = (bf16[3072,256]{1,0:T(8,128)(2,1)S(1)}, bf16[3072,256]{1,0:T(8,128)(2,1)}, u32[]{:S(2)}) copy-start(bf16[3072,256]{1,0:T(8,128)(2,1)} %get-tuple-element.8.rows_ref) | copy-start | bytes 4718596
  67.1 1.3 %copy-start.3 = (bf16[3072,256]{1,0:T(8,128)(2,1)}, bf16[3072,256]{1,0:T(8,128)(2,1)S(1)}, u32[]{:S(2)}) copy-start(bf16[3072,256]{1,0:T(8,128)(2,1)S(1)} %constant_dynamic-update-slice_fusion) | copy-start | bytes 4718596

commit v2 on v1

--- a/solution.py
+++ b/solution.py
@@ -27,65 +27,152 @@
     )
 
 
+def ring_neighbours(g, d, groups, peers):
+    spot = g * peers + d
+    after = lax.rem(spot + 1, groups * peers)
+    before = lax.rem(spot + groups * peers - 1, groups * peers)
+    return (after // peers, lax.rem(after, peers)), (before // peers, lax.rem(before, peers))
+
+
+def prepare_kernel(
+    groups, peers, basis_ref, tangents_ref, rim_ref, laid_ref, flat, spread, sems
+):
+    g, d = lax.axis_index("grp"), lax.axis_index("dom")
+    following, previous = ring_neighbours(g, d, groups, peers)
+    rim_rows = rim_ref.shape[0]
+    elems, width = flat.shape
+    lines = width // LANES
+    load = pltpu.make_async_copy(tangents_ref, flat, sems.at[0])
+    load.start()
+    barrier = pltpu.get_barrier_semaphore()
+    for device in (following, previous):
+        pl.semaphore_signal(barrier, inc=1, device_id=device, device_id_type=MESH)
+    pl.semaphore_wait(barrier, 2)
+    rim_copy = pltpu.make_async_remote_copy(
+        src_ref=basis_ref.at[pl.ds(0, rim_rows)], dst_ref=rim_ref,
+        send_sem=sems.at[1], recv_sem=sems.at[2], device_id=previous, device_id_type=MESH,
+    )
+    rim_copy.start()
+    load.wait()
+    for m in range(lines):
+        block = flat[:, m * LANES:(m + 1) * LANES].astype(jnp.float32)
+        spread[pl.ds(m, elems, stride=lines + 8), :] = block
+    for e in range(elems):
+        piece = spread[e * (lines + 8):e * (lines + 8) + lines, :]
+        laid_ref[e * lines:(e + 1) * lines, :] = piece.astype(jnp.bfloat16)
+    rim_copy.wait()
+
+
+def prepare(basis, tangents, rim_rows, groups, peers):
+    elems, width = tangents.shape
+    columns = basis.shape[1]
+    lines = width // LANES
+    vmem = pl.BlockSpec(memory_space=pltpu.VMEM)
+    whole = pl.BlockSpec(memory_space=pltpu.HBM)
+    return pl.pallas_call(
+        functools.partial(prepare_kernel, groups, peers),
+        out_shape=(
+            jax.ShapeDtypeStruct((rim_rows, columns), jnp.bfloat16),
+            jax.ShapeDtypeStruct((elems * lines, LANES), jnp.bfloat16),
+        ),
+        in_specs=[whole, whole],
+        out_specs=(vmem, vmem),
+        scratch_shapes=[
+            pltpu.VMEM((elems, width), jnp.bfloat16),
+            pltpu.VMEM((elems * (lines + 8), LANES), jnp.float32),
+            pltpu.SemaphoreType.DMA((3,)),
+        ],
+        compiler_params=pltpu.CompilerParams(
+            collective_id=1, has_side_effects=True, vmem_limit_bytes=VMEM_LIMIT
+        ),
+        name="prepare",
+    )(basis, tangents)
+
+
 def assemble_kernel(
-    own_rows, rim_rows, nodes_ref, weights_ref, basis_ref, rim_ref, tangents_ref,
-    rows_ref, edge_ref, over_ref, *scratch,
+    own_rows, rim_rows, nodes_ref, weights_ref, basis_hbm, rim_ref, laid_ref,
+    rows_ref, edge_ref, over_ref, basis_ref, basis_sem, *scratch,
 ):
     halves = basis_ref.shape[1] // LANES
-    table = scratch[:halves]
-    totals = [scratch[halves * (1 + u):halves * (2 + u)] for u in range(GROUP)]
-    at = halves * (1 + GROUP)
-    picked = [scratch[at + halves * u:at + halves * (u + 1)] for u in range(GROUP)]
-    at += halves * GROUP
-    products = [scratch[at + halves * u:at + halves * (u + 1)] for u in range(GROUP)]
+    taken = iter(scratch)
+
+    def buffers():
+        return [next(taken) for _ in range(halves)]
+
+    table = buffers()
+    totals = [buffers() for _ in range(GROUP)]
+    picked = [[buffers() for _ in range(GROUP)] for _ in range(2)]
+    products = [[buffers() for _ in range(GROUP)] for _ in range(2)]
     node_count, elem_count = nodes_ref.shape
+    lines = laid_ref.shape[0] // elem_count
     chunk = rim_rows
     all_rows = own_rows + rim_rows
+    load = pltpu.make_async_copy(basis_hbm, basis_ref, basis_sem)
+    load.start()
+
+    def clear(i, carry):
+        at_rows = pl.ds(pl.multiple_of(i * chunk, chunk), chunk)
+        for h in range(halves):
+            for u in range(GROUP):
+                totals[u][h][at_rows, :] = jnp.zeros((chunk, LANES), jnp.float32)
+        return carry
+
+    lax.fori_loop(0, all_rows // chunk, clear, 0)
+    for h in range(halves):
+        table[h][own_rows:all_rows, :] = rim_ref[:, h * LANES:(h + 1) * LANES].astype(jnp.float32)
+        table[h][all_rows:all_rows + 8, :] = jnp.zeros((8, LANES), jnp.float32)
+        for u in range(GROUP):
+            totals[u][h][all_rows:all_rows + 8, :] = jnp.zeros((8, LANES), jnp.float32)
+            for turn in range(2):
+                for buffer in (picked[turn][u][h], products[turn][u][h]):
+                    buffer[...] = jnp.zeros(buffer.shape, jnp.float32)
+    load.wait()
 
     def widen(i, carry):
         at_rows = pl.ds(pl.multiple_of(i * chunk, chunk), chunk)
         for h in range(halves):
             table[h][at_rows, :] = basis_ref[at_rows, h * LANES:(h + 1) * LANES].astype(jnp.float32)
+        return carry
+
+    lax.fori_loop(0, own_rows // chunk, widen, 0)
+    keep = lax.broadcasted_iota(jnp.int32, (8, LANES), 0) < 3
+
+    def scatter(turn, base):
+        for k in range(node_count):
             for u in range(GROUP):
-                totals[u][h][at_rows, :] = jnp.zeros((chunk, LANES), jnp.float32)
-        return carry
-
-    lax.fori_loop(0, own_rows // chunk, widen, 0)
-    for h in range(halves):
-        table[h][own_rows:all_rows, :] = rim_ref[:, h * LANES:(h + 1) * LANES].astype(jnp.float32)
-        table[h][all_rows:all_rows + 8, :] = jnp.zeros((8, LANES), jnp.float32)
-        for u in range(GROUP):
-            totals[u][h][own_rows:all_rows + 8, :] = jnp.zeros((rim_rows + 8, LANES), jnp.float32)
-    keep = lax.broadcasted_iota(jnp.int32, (8, LANES), 0) < 3
-
-    def add_group(i, carry):
-        base = i * GROUP
-        starts = [[nodes_ref[k, base + u] * 3 for k in range(node_count)] for u in range(GROUP)]
+                spot = pl.ds(nodes_ref[k, base + u] * 3, 8)
+                for h in range(halves):
+                    part = jnp.where(keep, products[turn][u][h][3 * k:3 * k + 8, :], 0.0)
+                    totals[u][h][spot, :] = totals[u][h][spot, :] + part
+
+    def multiply(turn, base):
         for u in range(GROUP):
             for k in range(node_count):
+                spot = pl.ds(nodes_ref[k, base + u] * 3, 8)
                 for h in range(halves):
-                    picked[u][h][3 * k:3 * k + 8, :] = table[h][pl.ds(starts[u][k], 8), :]
+                    picked[turn][u][h][3 * k:3 * k + 8, :] = table[h][spot, :]
         for u in range(GROUP):
-            block = jnp.concatenate([picked[u][h][:EDOF, :] for h in range(halves)], axis=1)
+            block = jnp.concatenate([picked[turn][u][h][:EDOF, :] for h in range(halves)], axis=1)
+            pairs = laid_ref[pl.ds(pl.multiple_of((base + u) * lines, lines), lines), :]
+            matrix = jnp.concatenate([pairs[:, :EDOF], pairs[:, EDOF:]], axis=0)
             product = jnp.dot(
-                tangents_ref[base + u], block.astype(jnp.bfloat16),
-                preferred_element_type=jnp.float32,
+                matrix, block.astype(jnp.bfloat16), preferred_element_type=jnp.float32
             ) * weights_ref[base + u]
             for h in range(halves):
-                products[u][h][:EDOF, :] = product[:, h * LANES:(h + 1) * LANES]
-        for k in range(node_count):
-            for u in range(GROUP):
-                for h in range(halves):
-                    part = jnp.where(keep, products[u][h][3 * k:3 * k + 8, :], 0.0)
-                    spot = pl.ds(starts[u][k], 8)
-                    totals[u][h][spot, :] = totals[u][h][spot, :] + part
-        return carry
-
-    for u in range(GROUP):
-        for h in range(halves):
-            picked[u][h][...] = jnp.zeros(picked[u][h].shape, jnp.float32)
-            products[u][h][...] = jnp.zeros(products[u][h].shape, jnp.float32)
-    lax.fori_loop(0, elem_count // GROUP, add_group, 0)
+                lanes = slice(h * LANES, (h + 1) * LANES)
+                products[turn][u][h][pl.ds(0, lines, stride=2), :] = product[:lines, lanes]
+                products[turn][u][h][pl.ds(1, lines, stride=2), :] = product[lines:, lanes]
+
+    def add_pair(i, carry):
+        base = i * (2 * GROUP)
+        multiply(0, base)
+        scatter(1, jnp.maximum(base - GROUP, 0))
+        multiply(1, base + GROUP)
+        scatter(0, base)
+        return carry
+
+    lax.fori_loop(0, elem_count // (2 * GROUP), add_pair, 0)
+    scatter(1, elem_count - GROUP)
 
     def summed(at_rows, h):
         value = totals[0][h][at_rows, :]
@@ -108,7 +195,7 @@
         over_ref[:, lanes] = summed(pl.ds(own_rows, rim_rows), h)
 
 
-def assemble(basis, rim_basis, tangents, nodes, weights):
+def assemble(basis, rim_basis, laid, nodes, weights):
     own_rows, columns = basis.shape
     rim_rows = rim_basis.shape[0]
     halves = columns // LANES
@@ -116,6 +203,7 @@
     short = pltpu.VMEM((EDOF + 8, LANES), jnp.float32)
     vmem = pl.BlockSpec(memory_space=pltpu.VMEM)
     smem = pl.BlockSpec(memory_space=pltpu.SMEM)
+    whole = pl.BlockSpec(memory_space=pltpu.HBM)
     return pl.pallas_call(
         functools.partial(assemble_kernel, own_rows, rim_rows),
         out_shape=(
@@ -123,17 +211,18 @@
             jax.ShapeDtypeStruct((rim_rows, columns), jnp.float32),
             jax.ShapeDtypeStruct((rim_rows, columns), jnp.float32),
         ),
-        in_specs=[smem, smem, vmem, vmem, vmem],
+        in_specs=[smem, smem, whole, vmem, vmem],
         out_specs=(vmem, vmem, vmem),
-        scratch_shapes=[tall] * (halves * (1 + GROUP)) + [short] * (halves * GROUP * 2),
+        scratch_shapes=[pltpu.VMEM((own_rows, columns), jnp.bfloat16), pltpu.SemaphoreType.DMA]
+        + [tall] * (halves * (1 + GROUP)) + [short] * (halves * GROUP * 4),
         compiler_params=pltpu.CompilerParams(vmem_limit_bytes=VMEM_LIMIT),
         name="assemble",
-    )(nodes, weights, basis, rim_basis, tangents)
+    )(nodes, weights, basis, rim_basis, laid)
 
 
 def reduce_kernel(
-    peers, factor, basis_ref, rows_ref, edge_ref, over_ref, out_ref, edge_out_ref,
-    arrived, part, half, shards, mine, rim_sems, pair_sems, send_sems, recv_sems,
+    peers, factor, basis_hbm, rows_hbm, edge_ref, over_ref, out_ref, edge_out_ref,
+    basis_ref, rows_ref, load_sems, arrived, part, half, shards, mine, rim_sems, pair_sems, send_sems, recv_sems,
     spread_sems, spread_recv, pass_sems, pass_recv,
 ):
     g = lax.axis_index("grp")
@@ -142,11 +231,13 @@
     rim_rows, columns = edge_ref.shape
     own_rows = basis_ref.shape[0]
     height = columns // peers
-    spot = g * peers + d
-    after = lax.rem(spot + 1, 2 * peers)
-    before = lax.rem(spot + 2 * peers - 1, 2 * peers)
-    following = (after // peers, lax.rem(after, peers))
-    previous = (before // peers, lax.rem(before, peers))
+    following, previous = ring_neighbours(g, d, 2, peers)
+    loads = [
+        pltpu.make_async_copy(basis_hbm, basis_ref, load_sems.at[0]),
+        pltpu.make_async_copy(rows_hbm, rows_ref, load_sems.at[1]),
+    ]
+    for load in loads:
+        load.start()
 
     def shard(of):
         return pl.ds(pl.multiple_of(of * height, height), height)
@@ -169,6 +260,8 @@
     rim_copy = remote(over_ref, arrived, rim_sems.at[0], rim_sems.at[1], following)
     rim_copy.start()
     part[...] = jnp.zeros(part.shape, jnp.float32)
+    for load in loads:
+        load.wait()
 
     def project(i, carry):
         at_rows = pl.ds(pl.multiple_of(i * rim_rows, rim_rows), rim_rows)
@@ -233,6 +326,7 @@
     rim_rows, columns = edge.shape
     height = columns // peers
     vmem = pl.BlockSpec(memory_space=pltpu.VMEM)
+    whole = pl.BlockSpec(memory_space=pltpu.HBM)
     dma = pltpu.SemaphoreType.DMA
     return pl.pallas_call(
         functools.partial(reduce_kernel, peers, factor),
@@ -240,9 +334,10 @@
             jax.ShapeDtypeStruct((2, columns, columns), jnp.float32),
             jax.ShapeDtypeStruct((rim_rows, columns), jnp.bfloat16),
         ),
-        in_specs=[vmem] * 4,
+        in_specs=[whole, whole, vmem, vmem],
         out_specs=(vmem, vmem),
         scratch_shapes=[
+            pltpu.VMEM(basis.shape, jnp.bfloat16), pltpu.VMEM(rows.shape, jnp.bfloat16), dma((2,)),
             pltpu.VMEM((rim_rows, columns), jnp.float32),
             pltpu.VMEM((2, columns, columns), jnp.float32),
             pltpu.VMEM((columns, columns), jnp.float32),
@@ -261,13 +356,10 @@
 def local(reduced_basis, tangents, connectivity, weights):
     own_rows, columns = reduced_basis.shape
     rim_rows = RIM * 3
-    elem_count = weights.shape[0]
     groups, peers = lax.axis_size("grp"), lax.axis_size("dom")
     factor = 1.0 / float(own_rows * groups * peers)
-    rim_basis = passed_along(reduced_basis[:rim_rows], ("grp", "dom"), -1)
-    rows, edge, over = assemble(
-        reduced_basis, rim_basis, tangents.reshape(elem_count, EDOF, EDOF), connectivity, weights
-    )
+    rim_basis, laid = prepare(reduced_basis, tangents, rim_rows, groups, peers)
+    rows, edge, over = assemble(reduced_basis, rim_basis, laid, connectivity, weights)
     if groups == 2 and columns % peers == 0 and (columns // peers) % 8 == 0:
         both, edge_rows = reduce_all(reduced_basis, rows, edge, over, peers, factor)
         return lax.dynamic_update_slice(rows, edge_rows, (0, 0)), both[0], both[1]

time: 68.6 us -> 69.8 us (1.017)
  Pallas kernels: 52.9 us -> 63.5 us
  local copies, waits for them, and re-layouts: 9.7 us -> 5.36 us
  waiting for transfers between devices: 3.8 us -> 0 us
  starting transfers between devices: 1.29 us -> 0 us
    pallas_call x0 -> x1, Pallas kernels: none -> 11.8 us  [prepare(): pl.pallas_call(functools.partial(prepare_kernel, groups, peers), out_shap...]
    ppermute x1 -> x0, waiting for transfers between devices: 3.8 us -> none  [passed_along(): return lax.ppermute(x, axis, pairs)]
    reshape x1 -> x0, local copies, waits for them, and re-layouts: 2.99 us -> none  [local(): tangents.reshape(elem_count, EDOF, EDOF)]
    ppermute x1 -> x0, starting transfers between devices: 1.29 us -> none  [passed_along(): return lax.ppermute(x, axis, pairs)]
    slice x1 -> x0, local copies, waits for them, and re-layouts: 0.94 us -> none  [local(): rim_basis = passed_along(reduced_basis[:rim_rows], ('grp', 'dom'), -1)]
    unnamed x13 -> x12, local copies, waits for them, and re-layouts: 4.86 us -> 4.44 us
  transfers between devices with their start and end apart: 1 -> 0, of which waited for: 1 -> 0; matrix products, arithmetic and copies ran while one was open for 7% -> 0% of each run, Pallas kernels for 0% -> 0%
where the time goes in v2:
time: 69.8 us; the launch traced here: 69.6 us
  Pallas kernels  63.5 us (91%)
  local copies, waits for them, and re-layouts  5.36 us (8%)
  between operations  0.71 us (1%)
    pallas_call x1, Pallas kernels, reduce_all(): pl.pallas_call(functools.partial(reduce_kernel, peers, factor), out_shape...  34.2 us
    pallas_call x1, Pallas kernels, assemble(): pl.pallas_call(functools.partial(assemble_kernel, own_rows, rim_rows), ou...  17.6 us
    pallas_call x1, Pallas kernels, prepare(): pl.pallas_call(functools.partial(prepare_kernel, groups, peers), out_shap...  11.8 us
    unnamed x12, local copies, waits for them, and re-layouts  4.44 us

profile of v2, /device:TPU:0, one launch (start us, length us, event | category | flops | bytes accessed | tf_op | source)
XLA Modules:
  0.0 69.6 jit_solution(425413405939292269)
XLA Ops:
  0.6 0.0 copy-start
  0.6 1.4 %copy-done = bf16[3072,256]{1,0:T(8,128)(2,1)S(1)} copy-done((bf16[3072,256]{1,0:T(8,128)(2,1)S(1)}, bf16[3072,256]{1,0:T(8,128)(2,1)}, u32[]{:S(2)}) %copy-start) | copy-done | bytes 1572888
  2.0 0.0 copy-start.3
  2.0 1.2 %copy-done.3 = bf16[128,4096]{1,0:T(8,128)(2,1)S(1)} copy-done((bf16[128,4096]{1,0:T(8,128)(2,1)S(1)}, bf16[128,4096]{1,0:T(8,128)(2,1)}, u32[]{:S(2)}) %copy-start.3) | copy-done | bytes 1048600
  3.3 0.0 copy-start.4
  3.3 0.0 copy-start.5
  3.3 11.8 %prepare.1 = (bf16[384,256]{1,0:T(8,128)(2,1)S(1)}, bf16[4096,128]{1,0:T(8,128)(2,1)S(1)}) custom-call(bf16[3072,256]{1,0:T(8,128)(2,1)S(1)} %copy-done, bf16[128,4096]{1,0:T(8,128)(2,1)S(1)} %copy-done.3), custom_call_target="tpu_custom_call" | custom-call | tf_op jit(solution)/shard_map/prepare/pallas_call | solution.py:72
  15.0 0.0 copy-done.4
  15.1 0.0 copy-done.5
  15.1 17.6 %assemble.1 = (bf16[3072,256]{1,0:T(8,128)(2,1)}, f32[384,256]{1,0:T(8,128)S(1)}, f32[384,256]{1,0:T(8,128)S(1)}) custom-call(s32[20,128]{1,0:T(8,128)S(1)} %copy-done.4, f32[128]{0:T(128)S(1)} %copy-done.5, bf16[3072,256]{1,0:T(8,128)(2,1)S(1)} %copy-done, bf16[384,256]{1,0:T(8,128)(2,1)S(1)} %get-tuple-element.10.rim_ref, ...), custom_call_target="tpu_custom_call" | custom-call | tf_op jit(solution)/shard_map/assemble/pallas_call | solution.py:207
  32.7 0.0 copy-start.1
  32.7 1.4 %copy-done.1 = bf16[3072,256]{1,0:T(8,128)(2,1)S(1)} copy-done((bf16[3072,256]{1,0:T(8,128)(2,1)S(1)}, bf16[3072,256]{1,0:T(8,128)(2,1)}, u32[]{:S(2)}) %copy-start.1) | copy-done | bytes 1572888
  34.1 34.2 %reduce_all.1 = (f32[2,256,256]{2,1,0:T(8,128)S(1)}, bf16[384,256]{1,0:T(8,128)(2,1)S(1)}) custom-call(bf16[3072,256]{1,0:T(8,128)(2,1)S(1)} %copy-done, bf16[3072,256]{1,0:T(8,128)(2,1)S(1)} %copy-done.1, f32[384,256]{1,0:T(8,128)S(1)} %get-tuple-element.13.edge_ref, f32[384,256]{1,0:T(8,128)S(1)} %get-tuple-element.14.over_ref), custom_call_target="tpu_custom_call" | custom-call | tf_op jit(solution)/shard_map/reduce_all/pallas_call | solution.py:331
  68.3 0.0 copy-start.2
  68.3 0.9 %slice_bitcast_fusion = (f32[256,256]{1,0:T(8,128)}, f32[256,256]{1,0:T(8,128)}) fusion(f32[2,256,256]{2,1,0:T(8,128)S(1)} %get-tuple-element.16), kind=kLoop, calls=%fused_computation | loop fusion | bytes 1048576 | tf_op jit(solution)/shard_map/squeeze | solution.py:365
  69.2 0.4 copy-done.2
  (1 shorter events, 0.0 us)
Async XLA Ops:
  0.6 1.4 %copy-start = (bf16[3072,256]{1,0:T(8,128)(2,1)S(1)}, bf16[3072,256]{1,0:T(8,128)(2,1)}, u32[]{:S(2)}) copy-start(bf16[3072,256]{1,0:T(8,128)(2,1)} %basis_hbm.3) | copy-start | bytes 4718596
  2.0 1.2 %copy-start.3 = (bf16[128,4096]{1,0:T(8,128)(2,1)S(1)}, bf16[128,4096]{1,0:T(8,128)(2,1)}, u32[]{:S(2)}) copy-start(bf16[128,4096]{1,0:T(8,128)(2,1)} %tangents_ref.1) | copy-start | bytes 3145732
  3.3 11.8 %copy-start.4 = (s32[20,128]{1,0:T(8,128)S(1)}, s32[20,128]{1,0:T(8,128)}, u32[]{:S(2)}) copy-start(s32[20,128]{1,0:T(8,128)} %nodes_ref.1) | copy-start | bytes 30724
  3.3 11.8 %copy-start.5 = (f32[128]{0:T(128)S(1)}, f32[128]{0:T(128)}, u32[]{:S(2)}) copy-start(f32[128]{0:T(128)} %weights_ref.1) | copy-start | bytes 1540
  32.7 1.4 %copy-start.1 = (bf16[3072,256]{1,0:T(8,128)(2,1)S(1)}, bf16[3072,256]{1,0:T(8,128)(2,1)}, u32[]{:S(2)}) copy-start(bf16[3072,256]{1,0:T(8,128)(2,1)} %get-tuple-element.12.rows_hbm) | copy-start | bytes 4718596
  68.3 1.3 %copy-start.2 = (bf16[3072,256]{1,0:T(8,128)(2,1)}, bf16[3072,256]{1,0:T(8,128)(2,1)S(1)}, u32[]{:S(2)}) copy-start(bf16[3072,256]{1,0:T(8,128)(2,1)S(1)} %constant_dynamic-update-slice_fusion) | copy-start | bytes 4718596

commit v3 on v2

--- a/solution.py
+++ b/solution.py
@@ -11,8 +11,10 @@
 RIM = 128
 LANES = 128
 GROUP = 4
+RIM_TYPE = jnp.bfloat16
+RIM_SCALE = 1.0
 MESH = pl.DeviceIdType.MESH
-VMEM_LIMIT = 48 * 1024 * 1024
+VMEM_LIMIT = 60 * 1024 * 1024
 
 
 def passed_along(x, axis, by):
@@ -31,28 +33,33 @@
     spot = g * peers + d
     after = lax.rem(spot + 1, groups * peers)
     before = lax.rem(spot + groups * peers - 1, groups * peers)
-    return (after // peers, lax.rem(after, peers)), (before // peers, lax.rem(before, peers))
+    following = (after // peers, lax.rem(after, peers))
+    previous = (before // peers, lax.rem(before, peers))
+    return spot, following, previous
 
 
 def prepare_kernel(
     groups, peers, basis_ref, tangents_ref, rim_ref, laid_ref, flat, spread, sems
 ):
     g, d = lax.axis_index("grp"), lax.axis_index("dom")
-    following, previous = ring_neighbours(g, d, groups, peers)
+    spot, following, previous = ring_neighbours(g, d, groups, peers)
+    has_next, has_previous = spot < groups * peers - 1, spot > 0
     rim_rows = rim_ref.shape[0]
     elems, width = flat.shape
     lines = width // LANES
     load = pltpu.make_async_copy(tangents_ref, flat, sems.at[0])
     load.start()
     barrier = pltpu.get_barrier_semaphore()
-    for device in (following, previous):
-        pl.semaphore_signal(barrier, inc=1, device_id=device, device_id_type=MESH)
-    pl.semaphore_wait(barrier, 2)
+    for present, device in ((has_next, following), (has_previous, previous)):
+        @pl.when(present)
+        def _(device=device):
+            pl.semaphore_signal(barrier, inc=1, device_id=device, device_id_type=MESH)
+    pl.semaphore_wait(barrier, has_next.astype(jnp.int32) + has_previous.astype(jnp.int32))
     rim_copy = pltpu.make_async_remote_copy(
         src_ref=basis_ref.at[pl.ds(0, rim_rows)], dst_ref=rim_ref,
         send_sem=sems.at[1], recv_sem=sems.at[2], device_id=previous, device_id_type=MESH,
     )
-    rim_copy.start()
+    pl.when(has_previous)(rim_copy.start)
     load.wait()
     for m in range(lines):
         block = flat[:, m * LANES:(m + 1) * LANES].astype(jnp.float32)
@@ -60,7 +67,13 @@
     for e in range(elems):
         piece = spread[e * (lines + 8):e * (lines + 8) + lines, :]
         laid_ref[e * lines:(e + 1) * lines, :] = piece.astype(jnp.bfloat16)
-    rim_copy.wait()
+    pl.when(has_next)(rim_copy.wait_recv)
+
+    @pl.when(jnp.logical_not(has_next))
+    def _():
+        rim_ref[...] = jnp.zeros(rim_ref.shape, rim_ref.dtype)
+
+    pl.when(has_previous)(rim_copy.wait_send)
 
 
 def prepare(basis, tangents, rim_rows, groups, peers):
@@ -192,7 +205,8 @@
         edge = summed(pl.ds(0, rim_rows), h)
         edge_ref[:, lanes] = edge
         rows_ref[0:rim_rows, lanes] = edge.astype(jnp.bfloat16)
-        over_ref[:, lanes] = summed(pl.ds(own_rows, rim_rows), h)
+        over = summed(pl.ds(own_rows, rim_rows), h)
+        over_ref[:, lanes] = (over * (1.0 / RIM_SCALE)).astype(over_ref.dtype)
 
 
 def assemble(basis, rim_basis, laid, nodes, weights):
@@ -209,7 +223,7 @@
         out_shape=(
             jax.ShapeDtypeStruct((own_rows, columns), jnp.bfloat16),
             jax.ShapeDtypeStruct((rim_rows, columns), jnp.float32),
-            jax.ShapeDtypeStruct((rim_rows, columns), jnp.float32),
+            jax.ShapeDtypeStruct((rim_rows, columns), RIM_TYPE),
         ),
         in_specs=[smem, smem, whole, vmem, vmem],
         out_specs=(vmem, vmem, vmem),
@@ -231,7 +245,8 @@
     rim_rows, columns = edge_ref.shape
     own_rows = basis_ref.shape[0]
     height = columns // peers
-    following, previous = ring_neighbours(g, d, 2, peers)
+    spot, following, previous = ring_neighbours(g, d, 2, peers)
+    has_next, has_previous = spot < 2 * peers - 1, spot > 0
     loads = [
         pltpu.make_async_copy(basis_hbm, basis_ref, load_sems.at[0]),
         pltpu.make_async_copy(rows_hbm, rows_ref, load_sems.at[1]),
@@ -246,10 +261,15 @@
         return lax.rem(d + k, peers)
 
     barrier = pltpu.get_barrier_semaphore()
-    greeted = [sibling, following, previous] + [(g, peer(k)) for k in range(1, peers)]
+    greeted = [sibling] + [(g, peer(k)) for k in range(1, peers)]
     for device in greeted:
         pl.semaphore_signal(barrier, inc=1, device_id=device, device_id_type=MESH)
-    pl.semaphore_wait(barrier, len(greeted))
+    for present, device in ((has_next, following), (has_previous, previous)):
+        @pl.when(present)
+        def _(device=device):
+            pl.semaphore_signal(barrier, inc=1, device_id=device, device_id_type=MESH)
+    ring = has_next.astype(jnp.int32) + has_previous.astype(jnp.int32)
+    pl.semaphore_wait(barrier, len(greeted) + ring)
 
     def remote(src, dst, send, recv, device):
         return pltpu.make_async_remote_copy(
@@ -258,7 +278,7 @@
         )
 
     rim_copy = remote(over_ref, arrived, rim_sems.at[0], rim_sems.at[1], following)
-    rim_copy.start()
+    pl.when(has_next)(rim_copy.start)
     part[...] = jnp.zeros(part.shape, jnp.float32)
     for load in loads:
         load.wait()
@@ -271,14 +291,21 @@
         return carry
 
     lax.fori_loop(1, own_rows // rim_rows, project, 0)
-    rim_copy.wait()
-    edge_rows = (edge_ref[...] + arrived[...]).astype(jnp.bfloat16)
+    pl.when(has_previous)(rim_copy.wait_recv)
+
+    @pl.when(jnp.logical_not(has_previous))
+    def _():
+        arrived[...] = jnp.zeros(arrived.shape, arrived.dtype)
+
+    incoming = arrived[...].astype(jnp.float32) * RIM_SCALE
+    edge_rows = (edge_ref[...] + incoming).astype(jnp.bfloat16)
     edge_out_ref[...] = edge_rows
     part[0] += transposed_dot(basis_ref[0:rim_rows, :], edge_rows)
     part[1] += transposed_dot(edge_rows, edge_rows)
 
     pair_copy = remote(part.at[1 - g], half, pair_sems.at[0], pair_sems.at[1], sibling)
     pair_copy.start()
+    pl.when(has_next)(rim_copy.wait_send)
     pair_copy.wait()
     half[...] = half[...] + part[g]
 
@@ -338,7 +365,7 @@
         out_specs=(vmem, vmem),
         scratch_shapes=[
             pltpu.VMEM(basis.shape, jnp.bfloat16), pltpu.VMEM(rows.shape, jnp.bfloat16), dma((2,)),
-            pltpu.VMEM((rim_rows, columns), jnp.float32),
+            pltpu.VMEM((rim_rows, columns), RIM_TYPE),
             pltpu.VMEM((2, columns, columns), jnp.float32),
             pltpu.VMEM((columns, columns), jnp.float32),
             pltpu.VMEM((peers, height, columns), jnp.float32),
@@ -363,7 +390,7 @@
     if groups == 2 and columns % peers == 0 and (columns // peers) % 8 == 0:
         both, edge_rows = reduce_all(reduced_basis, rows, edge, over, peers, factor)
         return lax.dynamic_update_slice(rows, edge_rows, (0, 0)), both[0], both[1]
-    incoming = passed_along(over, ("grp", "dom"), 1)
+    incoming = passed_along(over, ("grp", "dom"), 1).astype(jnp.float32) * RIM_SCALE
     edge_rows = (edge + incoming).astype(jnp.bfloat16)
     rows = lax.dynamic_update_slice(rows, edge_rows, (0, 0))
     sums = lax.psum(

time: 69.8 us -> 64.5 us (0.924)
  Pallas kernels: 63.5 us -> 60.2 us
  local copies, waits for them, and re-layouts: 5.36 us -> 3.47 us
    unnamed x12 -> x0, local copies, waits for them, and re-layouts: 4.44 us -> none
    pallas_call x1, Pallas kernels: 34.2 us -> 31 us  [reduce_all(): pl.pallas_call(functools.partial(reduce_kernel, peers, factor), out_shape...]
    dynamic_update_slice x1, local copies, waits for them, and re-layouts: 0.02 us -> 1.62 us  [local(): return (lax.dynamic_update_slice(rows, edge_rows, (0, 0)), both[0], both[1])]
    pallas_call x1, Pallas kernels: 11.8 us -> 10.4 us  [prepare(): pl.pallas_call(functools.partial(prepare_kernel, groups, peers), out_shap...]
    pallas_call x1, Pallas kernels: 17.6 us -> 18.8 us  [assemble(): pl.pallas_call(functools.partial(assemble_kernel, own_rows, rim_rows), ou...]
    squeeze x1, local copies, waits for them, and re-layouts: 0.9 us -> 1.85 us  [local(): return (lax.dynamic_update_slice(rows, edge_rows, (0, 0)), both[0], both[1])]
where the time goes in v3:
time: 64.5 us; the launch traced here: 64.3 us
  Pallas kernels  60.2 us (93%)
  local copies, waits for them, and re-layouts  3.47 us (5%)
  between operations  0.65 us (1%)
    pallas_call x1, Pallas kernels, reduce_all(): pl.pallas_call(functools.partial(reduce_kernel, peers, factor), out_shape...  31 us
    pallas_call x1, Pallas kernels, assemble(): pl.pallas_call(functools.partial(assemble_kernel, own_rows, rim_rows), ou...  18.8 us
    pallas_call x1, Pallas kernels, prepare(): pl.pallas_call(functools.partial(prepare_kernel, groups, peers), out_shap...  10.4 us
    squeeze x1, local copies, waits for them, and re-layouts, local(): return (lax.dynamic_update_slice(rows, edge_rows, (0, 0)), both[0], both[1])  1.85 us
    dynamic_update_slice x1, local copies, waits for them, and re-layouts, local(): return (lax.dynamic_update_slice(rows, edge_rows, (0, 0)), both[0], both[1])  1.62 us

profile of v3, /device:TPU:0, one launch (start us, length us, event | category | flops | bytes accessed | tf_op | source)
XLA Modules:
  0.0 64.3 jit_solution(10896593948091346086)
XLA Ops:
  0.6 10.4 %prepare.1 = (bf16[384,256]{1,0:T(8,128)(2,1)}, bf16[4096,128]{1,0:T(8,128)(2,1)}) custom-call(bf16[3072,256]{1,0:T(8,128)(2,1)} %basis_hbm.3, bf16[128,4096]{1,0:T(8,128)(2,1)} %tangents_ref.1), custom_call_target="tpu_custom_call" | custom-call | tf_op jit(solution)/shard_map/prepare/pallas_call | solution.py:85
  11.0 18.8 %assemble.1 = (bf16[3072,256]{1,0:T(8,128)(2,1)}, f32[384,256]{1,0:T(8,128)}, bf16[384,256]{1,0:T(8,128)(2,1)}) custom-call(s32[20,128]{1,0:T(8,128)} %nodes_ref.1, f32[128]{0:T(128)} %weights_ref.1, bf16[3072,256]{1,0:T(8,128)(2,1)} %basis_hbm.3, bf16[384,256]{1,0:T(8,128)(2,1)} %get-tuple-element.10.rim_ref, bf16[4096,128]{1,0:T(8,128)(2,1)} %get-tuple-element.11.laid_ref), custom_call_target="tpu_custom_call" | custom-call | tf_op jit(solution)/shard_map/assemble/pallas_call | solution.py:221
  29.8 31.0 %reduce_all.1 = (f32[2,256,256]{2,1,0:T(8,128)}, bf16[384,256]{1,0:T(8,128)(2,1)}) custom-call(bf16[3072,256]{1,0:T(8,128)(2,1)} %basis_hbm.3, bf16[3072,256]{1,0:T(8,128)(2,1)} %get-tuple-element.12.rows_hbm, f32[384,256]{1,0:T(8,128)} %get-tuple-element.13.edge_ref, bf16[384,256]{1,0:T(8,128)(2,1)} %get-tuple-element.14.over_ref), custom_call_target="tpu_custom_call" | custom-call | tf_op jit(solution)/shard_map/reduce_all/pallas_call | solution.py:358
  60.8 1.6 %constant_dynamic-update-slice_fusion = bf16[3072,256]{1,0:T(8,128)(2,1)} fusion(bf16[3072,256]{1,0:T(8,128)(2,1)} %get-tuple-element.12.rows_hbm, bf16[384,256]{1,0:T(8,128)(2,1)} %get-tuple-element.15), kind=kLoop, calls=%fused_computation.2 | loop fusion | bytes 393216 | tf_op jit(solution)/shard_map/dynamic_update_slice | solution.py:392
  62.5 1.9 %slice_bitcast_fusion = (f32[256,256]{1,0:T(8,128)}, f32[256,256]{1,0:T(8,128)}) fusion(f32[2,256,256]{2,1,0:T(8,128)} %get-tuple-element.16), kind=kLoop, calls=%fused_computation | loop fusion | bytes 1048576 | tf_op jit(solution)/shard_map/squeeze | solution.py:392

commit v4 on v3

--- a/solution.py
+++ b/solution.py
@@ -149,13 +149,14 @@
 
     lax.fori_loop(0, own_rows // chunk, widen, 0)
     keep = lax.broadcasted_iota(jnp.int32, (8, LANES), 0) < 3
+    zero = jnp.minimum(nodes_ref[0, 0], 0)
 
     def scatter(turn, base):
         for k in range(node_count):
             for u in range(GROUP):
                 spot = pl.ds(nodes_ref[k, base + u] * 3, 8)
                 for h in range(halves):
-                    part = jnp.where(keep, products[turn][u][h][3 * k:3 * k + 8, :], 0.0)
+                    part = jnp.where(keep, products[turn][u][h][pl.ds(zero + 3 * k, 8), :], 0.0)
                     totals[u][h][spot, :] = totals[u][h][spot, :] + part
 
     def multiply(turn, base):
@@ -163,7 +164,7 @@
             for k in range(node_count):
                 spot = pl.ds(nodes_ref[k, base + u] * 3, 8)
                 for h in range(halves):
-                    picked[turn][u][h][3 * k:3 * k + 8, :] = table[h][spot, :]
+                    picked[turn][u][h][pl.ds(zero + 3 * k, 8), :] = table[h][spot, :]
         for u in range(GROUP):
             block = jnp.concatenate([picked[turn][u][h][:EDOF, :] for h in range(halves)], axis=1)
             pairs = laid_ref[pl.ds(pl.multiple_of((base + u) * lines, lines), lines), :]
@@ -236,7 +237,7 @@
 
 def reduce_kernel(
     peers, factor, basis_hbm, rows_hbm, edge_ref, over_ref, out_ref, edge_out_ref,
-    basis_ref, rows_ref, load_sems, arrived, part, half, shards, mine, rim_sems, pair_sems, send_sems, recv_sems,
+    basis_ref, rows_ref, load_sems, arrived, wide, part, half, shards, mine, rim_sems, pair_sems, send_sems, recv_sems,
     spread_sems, spread_recv, pass_sems, pass_recv,
 ):
     g = lax.axis_index("grp")
@@ -279,15 +280,14 @@
 
     rim_copy = remote(over_ref, arrived, rim_sems.at[0], rim_sems.at[1], following)
     pl.when(has_next)(rim_copy.start)
-    part[...] = jnp.zeros(part.shape, jnp.float32)
+    wide[...] = jnp.zeros(wide.shape, jnp.float32)
     for load in loads:
         load.wait()
 
     def project(i, carry):
         at_rows = pl.ds(pl.multiple_of(i * rim_rows, rim_rows), rim_rows)
         rows = rows_ref[at_rows, :]
-        part[0] += transposed_dot(basis_ref[at_rows, :], rows)
-        part[1] += transposed_dot(rows, rows)
+        wide[...] += transposed_dot(rows, jnp.concatenate([basis_ref[at_rows, :], rows], axis=1))
         return carry
 
     lax.fori_loop(1, own_rows // rim_rows, project, 0)
@@ -300,8 +300,11 @@
     incoming = arrived[...].astype(jnp.float32) * RIM_SCALE
     edge_rows = (edge_ref[...] + incoming).astype(jnp.bfloat16)
     edge_out_ref[...] = edge_rows
-    part[0] += transposed_dot(basis_ref[0:rim_rows, :], edge_rows)
-    part[1] += transposed_dot(edge_rows, edge_rows)
+    wide[...] += transposed_dot(
+        edge_rows, jnp.concatenate([basis_ref[0:rim_rows, :], edge_rows], axis=1)
+    )
+    part[0] = wide[:, :columns].T
+    part[1] = wide[:, columns:]
 
     pair_copy = remote(part.at[1 - g], half, pair_sems.at[0], pair_sems.at[1], sibling)
     pair_copy.start()
@@ -366,6 +369,7 @@
         scratch_shapes=[
             pltpu.VMEM(basis.shape, jnp.bfloat16), pltpu.VMEM(rows.shape, jnp.bfloat16), dma((2,)),
             pltpu.VMEM((rim_rows, columns), RIM_TYPE),
+            pltpu.VMEM((columns, 2 * columns), jnp.float32),
             pltpu.VMEM((2, columns, columns), jnp.float32),
             pltpu.VMEM((columns, columns), jnp.float32),
             pltpu.VMEM((peers, height, columns), jnp.float32),

time: 64.5 us -> 62.9 us (0.975)
  Pallas kernels: 60.2 us -> 58.5 us
    pallas_call x1, Pallas kernels: 18.8 us -> 17.1 us  [assemble(): pl.pallas_call(functools.partial(assemble_kernel, own_rows, rim_rows), ou...]
where the time goes in v4:
time: 62.9 us; the launch traced here: 62.7 us
  Pallas kernels  58.5 us (93%)
  local copies, waits for them, and re-layouts  3.47 us (6%)
  between operations  0.65 us (1%)
    pallas_call x1, Pallas kernels, reduce_all(): pl.pallas_call(functools.partial(reduce_kernel, peers, factor), out_shape...  31 us
    pallas_call x1, Pallas kernels, assemble(): pl.pallas_call(functools.partial(assemble_kernel, own_rows, rim_rows), ou...  17.1 us
    pallas_call x1, Pallas kernels, prepare(): pl.pallas_call(functools.partial(prepare_kernel, groups, peers), out_shap...  10.4 us
    squeeze x1, local copies, waits for them, and re-layouts, local(): return (lax.dynamic_update_slice(rows, edge_rows, (0, 0)), both[0], both[1])  1.85 us
    dynamic_update_slice x1, local copies, waits for them, and re-layouts, local(): return (lax.dynamic_update_slice(rows, edge_rows, (0, 0)), both[0], both[1])  1.62 us

profile of v4, /device:TPU:0, one launch (start us, length us, event | category | flops | bytes accessed | tf_op | source)
XLA Modules:
  0.0 62.7 jit_solution(18092607165807085590)
XLA Ops:
  0.6 10.4 %prepare.1 = (bf16[384,256]{1,0:T(8,128)(2,1)}, bf16[4096,128]{1,0:T(8,128)(2,1)}) custom-call(bf16[3072,256]{1,0:T(8,128)(2,1)} %basis_hbm.3, bf16[128,4096]{1,0:T(8,128)(2,1)} %tangents_ref.1), custom_call_target="tpu_custom_call" | custom-call | tf_op jit(solution)/shard_map/prepare/pallas_call | solution.py:85
  11.0 17.1 %assemble.1 = (bf16[3072,256]{1,0:T(8,128)(2,1)}, f32[384,256]{1,0:T(8,128)}, bf16[384,256]{1,0:T(8,128)(2,1)}) custom-call(s32[20,128]{1,0:T(8,128)} %nodes_ref.1, f32[128]{0:T(128)} %weights_ref.1, bf16[3072,256]{1,0:T(8,128)(2,1)} %basis_hbm.3, bf16[384,256]{1,0:T(8,128)(2,1)} %get-tuple-element.10.rim_ref, bf16[4096,128]{1,0:T(8,128)(2,1)} %get-tuple-element.11.laid_ref), custom_call_target="tpu_custom_call" | custom-call | tf_op jit(solution)/shard_map/assemble/pallas_call | solution.py:222
  28.1 31.0 %reduce_all.1 = (f32[2,256,256]{2,1,0:T(8,128)}, bf16[384,256]{1,0:T(8,128)(2,1)}) custom-call(bf16[3072,256]{1,0:T(8,128)(2,1)} %basis_hbm.3, bf16[3072,256]{1,0:T(8,128)(2,1)} %get-tuple-element.12.rows_hbm, f32[384,256]{1,0:T(8,128)} %get-tuple-element.13.edge_ref, bf16[384,256]{1,0:T(8,128)(2,1)} %get-tuple-element.14.over_ref), custom_call_target="tpu_custom_call" | custom-call | tf_op jit(solution)/shard_map/reduce_all/pallas_call | solution.py:361
  59.2 1.6 %constant_dynamic-update-slice_fusion = bf16[3072,256]{1,0:T(8,128)(2,1)} fusion(bf16[3072,256]{1,0:T(8,128)(2,1)} %get-tuple-element.12.rows_hbm, bf16[384,256]{1,0:T(8,128)(2,1)} %get-tuple-element.15), kind=kLoop, calls=%fused_computation.2 | loop fusion | bytes 393216 | tf_op jit(solution)/shard_map/dynamic_update_slice | solution.py:396
  60.8 1.9 %slice_bitcast_fusion = (f32[256,256]{1,0:T(8,128)}, f32[256,256]{1,0:T(8,128)}) fusion(f32[2,256,256]{2,1,0:T(8,128)} %get-tuple-element.16), kind=kLoop, calls=%fused_computation | loop fusion | bytes 1048576 | tf_op jit(solution)/shard_map/squeeze | solution.py:396
